TPU v7x, 512 devices: a whole 4x4x16 slice. The times are simulated.
512 devices in a mesh: dp: 16 (over z), expert: 32 (over y, x, core).
Axes of the slice: x: 4, y: 4, z: 16, core: 2. Of those that a mesh axis runs over, the one named last changes fastest.
Arguments:
- tokens: bfloat16 [65536, 1024], P(('dp', 'expert')), may hold values from -6 to 6
- grad_out: bfloat16 [65536, 1024], P(('dp', 'expert')), may hold values from -6 to 6
- expert_ids: int32 [65536, 2], P(('dp', 'expert')), may hold values from 0 to 31, all different within a row; in each aligned block of 128 rows (0 to 127, 128 to 255, ...) at most 16 rows name the same one
- route_probs: bfloat16 [65536, 2], P(('dp', 'expert')), may hold values from 0.19921875 to 1
- gate_up_weight: bfloat16 [1024, 32, 1536], P('dp', 'expert'), may hold values from -0.1875 to 0.1875
- down_weight: bfloat16 [32, 768, 1024], P('expert'), may hold values from -0.21875 to 0.21875
- gate_up_scale_index: int32 [8, 32, 2], P(None, 'expert'), may hold values from 0 to 15
- down_scale_index: int32 [32, 6], P('expert'), may hold values from 0 to 15
- scale_table: float32 [16], replicated, may hold values from 0.5 to 2
Outputs:
- token_grad: bfloat16 [65536, 1024], P(('dp', 'expert'))
- prob_grad: float32 [65536, 2], P(('dp', 'expert'))
- gate_up_grad: bfloat16 [1024, 32, 1536], P('dp', 'expert')
- down_grad: bfloat16 [32, 768, 1024], P('expert')
Inputs may be any that keep to these rules, and one draw needn't show every extreme that they name: `expert_ids`: each row names two different experts. The 128 rows of one device name one expert at most 16 times, and in every draw some device's rows name some expert exactly 16 times.
All inputs are finite; a program needn't handle non-finite values.
Results may differ from a plain program's by a relative error of at most 0.022.
Values may be sent and summed in bfloat16 or wider, within the bound.
No kernel may reach another device: no remote copies, remote signals or barrier semaphores. Data moves between devices by JAX's collectives and lax.ppermute only.
A program may use at most 64 MiB of HBM per device.

v0:
```python
import jax
import jax.numpy as jnp
from jax import lax
from jax.sharding import PartitionSpec as P

QBLOCK = 128


def lookup(level_index, level_table):
    onehot = (level_index[..., None] == jnp.arange(level_table.shape[0], dtype=jnp.int32)).astype(
        level_table.dtype
    )
    return jnp.sum(onehot * level_table, axis=-1)


def slot_tables(routes, experts, capacity):
    flat_routes = routes.reshape(-1)
    expert_hits = (flat_routes[:, None] == jnp.arange(experts, dtype=jnp.int32)[None, :]).astype(
        jnp.int32
    )
    before = jnp.cumsum(expert_hits, axis=0) - expert_hits
    slot_rank = jnp.sum(before * expert_hits, axis=1)
    destination = flat_routes * capacity + slot_rank
    table_hits = destination[:, None] == jnp.arange(experts * capacity, dtype=jnp.int32)[None, :]
    return table_hits.astype(jnp.float32).reshape(routes.shape[0], 2, experts * capacity)


def body(
    tokens,
    grad_out,
    expert_ids,
    route_probs,
    gate_up_weight,
    down_weight,
    gate_up_scale_index,
    down_scale_index,
    scale_table,
):
    high = lax.Precision.HIGHEST
    f32 = jnp.float32
    groups = lax.axis_size("expert")
    tok_dev = tokens.shape[0]
    model_width = tokens.shape[1]
    per_device = down_weight.shape[0]
    hidden = down_weight.shape[1]
    experts = per_device * groups
    capacity = 4 * tok_dev // experts
    slots_all = experts * capacity
    slot_hits = slot_tables(expert_ids, experts, capacity)
    either = (slot_hits[:, 0] + slot_hits[:, 1]).astype(jnp.bfloat16)
    row_shape = (groups, per_device, capacity, model_width)
    send_tokens = (
        jnp.einsum("ts,td->sd", either, tokens, preferred_element_type=f32)
        .astype(jnp.bfloat16)
        .reshape(row_shape)
    )
    send_grads = (
        jnp.einsum("ts,td->sd", either, grad_out, preferred_element_type=f32)
        .astype(jnp.bfloat16)
        .reshape(row_shape)
    )
    send_probs = (
        jnp.einsum("tks,tk->s", slot_hits, route_probs.astype(f32), precision=high)
        .astype(jnp.bfloat16)
        .reshape(row_shape[:3])
    )
    recv_tokens, recv_grads, recv_probs = (
        lax.all_to_all(send_tokens, "expert", split_axis=0, concat_axis=0, tiled=True),
        lax.all_to_all(send_grads, "expert", split_axis=0, concat_axis=0, tiled=True),
        lax.all_to_all(send_probs, "expert", split_axis=0, concat_axis=0, tiled=True),
    )
    level_rows = jnp.repeat(lookup(gate_up_scale_index, scale_table), QBLOCK, axis=0)
    full_scale = jnp.repeat(level_rows, hidden, axis=2)
    down_scale = jnp.repeat(lookup(down_scale_index, scale_table), QBLOCK, axis=1)
    down_eff = (down_weight.astype(f32) * down_scale[:, :, None]).astype(jnp.bfloat16)
    gathered = lax.all_gather(gate_up_weight, "dp", axis=0, tiled=True)
    gate_up_eff = (gathered.astype(f32) * full_scale).astype(jnp.bfloat16)
    projected = jnp.einsum("sjcd,djf->sjcf", recv_tokens, gate_up_eff, preferred_element_type=f32)
    gate_part = projected[..., :hidden]
    up_part = projected[..., hidden:]
    sigmoid_gate = jax.nn.sigmoid(gate_part)
    activated = gate_part * sigmoid_gate
    hidden_rows = (activated * up_part).astype(jnp.bfloat16)
    hidden_grad = jnp.einsum("sjcd,jfd->sjcf", recv_grads, down_eff, preferred_element_type=f32)
    probs_wide = recv_probs.astype(f32)[..., None]
    scaled_grad = probs_wide * hidden_grad
    gate_grad = scaled_grad * up_part * sigmoid_gate * (1.0 + gate_part * (1.0 - sigmoid_gate))
    up_grad = scaled_grad * activated
    joint_grad = jnp.concatenate([gate_grad, up_grad], axis=-1).astype(jnp.bfloat16)
    row_grads = jnp.einsum(
        "sjcf,djf->sjcd", joint_grad, gate_up_eff, preferred_element_type=f32
    ).astype(jnp.bfloat16)
    back_rows = lax.all_to_all(row_grads, "expert", split_axis=0, concat_axis=0, tiled=True)
    token_grad = jnp.dot(
        either, back_rows.reshape(slots_all, model_width), preferred_element_type=f32
    ).astype(jnp.bfloat16)
    expert_out = jnp.einsum("sjcf,jfd->sjcd", hidden_rows, down_eff, preferred_element_type=f32)
    back_out = lax.all_to_all(
        expert_out.astype(jnp.bfloat16), "expert", split_axis=0, concat_axis=0, tiled=True
    ).astype(expert_out.dtype)
    picked = jnp.einsum(
        "tks,sd->tkd", slot_hits, back_out.reshape(slots_all, model_width), precision=high
    )
    prob_grad = jnp.sum(picked * grad_out.astype(f32)[:, None, :], axis=-1)
    weighted = (probs_wide * hidden_rows.astype(f32)).astype(jnp.bfloat16)
    partial_sum = jnp.einsum("sjcd,sjcf->djf", recv_tokens, joint_grad, preferred_element_type=f32)
    gate_up_grad = lax.psum_scatter(
        (partial_sum * full_scale).astype(jnp.bfloat16), "dp", scatter_dimension=0, tiled=True
    )
    down_part = (
        jnp.einsum("sjcf,sjcd->jfd", weighted, recv_grads, preferred_element_type=f32)
        * down_scale[:, :, None]
    )
    down_grad = lax.psum(down_part.astype(jnp.bfloat16), "dp")
    return (token_grad, prob_grad, gate_up_grad, down_grad)


def solution(mesh):
    in_specs = (
        P(("dp", "expert"), None),
        P(("dp", "expert"), None),
        P(("dp", "expert"), None),
        P(("dp", "expert"), None),
        P("dp", "expert", None),
        P("expert", None, None),
        P(None, "expert", None),
        P("expert", None),
        P(),
    )
    out_specs = (
        P(("dp", "expert"), None),
        P(("dp", "expert"), None),
        P("dp", "expert", None),
        P("expert", None, None),
    )
    return jax.shard_map(body, mesh=mesh, in_specs=in_specs, out_specs=out_specs, check_vma=False)
```

profile of v0, /device:TPU:2, one launch (start us, length us, event | category | flops | bytes accessed | tf_op | source)
XLA Modules:
  0.0 354.2 jit_solution(2820792020950934844)
XLA Ops:
  12.5 9.4 %all-to-all-start = ((bf16[32,1,16]{2,1,0:T(2,128)(2,1)}), bf16[32,1,16]{2,1,0:T(2,128)(2,1)S(1)}, u32[]{:S(2)}, u32[]{:S(2)}) async-start(bf16[32,1,16]{2,1,0:T(2,128)(2,1)} %reshape.263), calls=%async_computation | async-start | bytes 32768 | tf_op jit(solution)/shard_map/all_to_all | solution.py:70
  23.5 4.5 %all-to-all-done = bf16[32,1,16]{2,1,0:T(2,128)(2,1)S(1)} async-done(((bf16[32,1,16]{2,1,0:T(2,128)(2,1)}), bf16[32,1,16]{2,1,0:T(2,128)(2,1)S(1)}, u32[]{:S(2)}, u32[]{:S(2)}) %all-to-all-start) | async-done | bytes 1056 | tf_op jit(solution)/shard_map/all_to_all | solution.py:70
  28.0 5.7 %all-to-all-start.2 = ((bf16[32,1,16,1024]{3,2,1,0:T(8,128)(2,1)}), bf16[32,1,16,1024]{3,2,1,0:T(8,128)(2,1)}, u32[]{:S(2)}, u32[]{:S(2)}) async-start(bf16[32,1,16,1024]{3,2,1,0:T(8,128)(2,1)} %bitcast.20), calls=%async_computation.2 | async-start | bytes 2097152 | tf_op jit(solution)/shard_map/all_to_all | solution.py:68
  36.4 54.6 %all-gather.2.cloned.1.call-done = bf16[1024,1,1536]{2,0,1:T(8,128)(2,1)} async-done(((bf16[64,1,1536]{2,0,1:T(8,128)(2,1)}), bf16[1024,1,1536]{2,0,1:T(8,128)(2,1)}) %all-gather.2.cloned.1.call-update) | async-done | bytes 3145744 | tf_op jit(solution)/shard_map/all_gather | solution.py:76
  91.0 3.2 copy.84
  94.2 7.4 %all-to-all-start.1 = ((bf16[32,1,16,1024]{3,2,1,0:T(8,128)(2,1)}), bf16[32,1,16,1024]{3,2,1,0:T(8,128)(2,1)}, u32[]{:S(2)}, u32[]{:S(2)}) async-start(bf16[32,1,16,1024]{3,2,1,0:T(8,128)(2,1)} %bitcast.158), calls=%async_computation.1 | async-start | bytes 2097152 | tf_op jit(solution)/shard_map/all_to_all | solution.py:69
  103.9 1.7 copy-done.1
  105.5 1.7 copy-done.2
  107.3 5.1 %convolution_bitcast_fusion = f32[32,1,16,1536]{3,0,2,1:T(8,128)} fusion(bf16[1024,1536,1]{0,1,2:T(8,128)(2,1)S(1)} %fusion.3, bf16[32,1,16,1024]{3,2,1,0:T(8,128)(2,1)} %all-to-all-done.2), kind=kOutput, calls=%fused_computation.4 | convolution fusion | flops 1610612736 | bytes 7340032 | tf_op jit(solution)/shard_map/sjcd,djf->sjcf/dot_general | solution.py:78
  112.3 5.5 %all-to-all-done.1 = bf16[32,1,16,1024]{3,2,1,0:T(8,128)(2,1)} async-done(((bf16[32,1,16,1024]{3,2,1,0:T(8,128)(2,1)}), bf16[32,1,16,1024]{3,2,1,0:T(8,128)(2,1)}, u32[]{:S(2)}, u32[]{:S(2)}) %all-to-all-start.1) | async-done | bytes 1048608 | tf_op jit(solution)/shard_map/all_to_all | solution.py:69
  117.8 5.3 %fusion.29 = (bf16[32,16,768]{2,0,1:T(8,128)(2,1)S(1)}, bf16[32,16,768]{2,0,1:T(8,128)(2,1)S(1)}, bf16[32,1,16,768]{3,0,2,1:T(8,128)(2,1)}) fusion(f32[32,1,16,1536]{3,0,2,1:T(8,128)} %convolution_bitcast_fusion, bf16[32,1,16,1024]{3,2,1,0:T(8,128)(2,1)} %all-to-all-done.1, bf16[1,768,1024]{2,1,0:T(8,128)(2,1)S(1)} %copy-done.11, f32[768]{0:T(1024)S(1)} %copy-done.8, ...), kind=kOutput, calls=%fused_computation.46 | convolution fusion | flops 813957120 | bytes 8131584 | tf_op jit(solution)/shard_map/sjcd,jfd->sjcf/dot_general | solution.py:84
  123.2 3.8 %fusion.15 = f32[1536,1024,1]{1,0,2:T(8,128)S(1)} fusion(bf16[32,16,768]{2,0,1:T(8,128)(2,1)S(1)} %get-tuple-element.25, bf16[32,16,768]{2,0,1:T(8,128)(2,1)S(1)} %get-tuple-element.24, bf16[32,1,16,1024]{3,2,1,0:T(8,128)(2,1)} %all-to-all-done.2), kind=kOutput, calls=%fused_computation.33 | convolution fusion | flops 1613758464 | bytes 8912896 | tf_op jit(solution)/shard_map/sjcd,sjcf->djf/dot_general | solution.py:106
  127.0 1.8 fusion.2
  128.8 3.0 copy.104
  136.0 5.7 %all-to-all-start.4 = ((bf16[32,1,16,1024]{3,2,1,0:T(8,128)(2,1)}), bf16[32,1,16,1024]{3,2,1,0:T(8,128)(2,1)}, u32[]{:S(2)}, u32[]{:S(2)}) async-start(bf16[32,1,16,1024]{3,2,1,0:T(8,128)(2,1)} %copy.94), calls=%async_computation.4 | async-start | bytes 2097152 | tf_op jit(solution)/shard_map/all_to_all | solution.py:98
  142.0 4.1 %fusion.11 = bf16[1,768,1024]{2,1,0:T(8,128)(2,1)} fusion(f32[768]{0:T(1024)S(1)} %copy-done.8, bf16[32,1,16,1024]{3,2,1,0:T(8,128)(2,1)} %all-to-all-done.1, bf16[32,1,16,768]{3,0,2,1:T(8,128)(2,1)} %get-tuple-element.26, f32[32,16]{0,1:T(8,128)S(1)} %copy.86), kind=kOutput, calls=%fused_computation.23 | convolution fusion | flops 808058880 | bytes 3412992 | tf_op jit(solution)/shard_map/sjcf,sjcd->jfd/dot_general | solution.py:111
  146.2 3.2 fusion.13
  150.9 7.1 %all-to-all-done.4 = bf16[32,1,16,1024]{3,2,1,0:T(8,128)(2,1)} async-done(((bf16[32,1,16,1024]{3,2,1,0:T(8,128)(2,1)}), bf16[32,1,16,1024]{3,2,1,0:T(8,128)(2,1)}, u32[]{:S(2)}, u32[]{:S(2)}) %all-to-all-start.4) | async-done | bytes 1048608 | tf_op jit(solution)/shard_map/all_to_all | solution.py:98
  158.0 5.0 %all-to-all-start.3 = ((bf16[32,1,16,1024]{3,2,1,0:T(8,128)(2,1)}), bf16[32,1,16,1024]{3,2,1,0:T(8,128)(2,1)S(1)}, u32[]{:S(2)}, u32[]{:S(2)}) async-start(bf16[32,1,16,1024]{3,2,1,0:T(8,128)(2,1)} %copy.93), calls=%async_computation.3 | async-start | bytes 2097152 | tf_op jit(solution)/shard_map/all_to_all | solution.py:93
  163.1 2.4 fusion.14
  165.5 13.8 %all-to-all-done.3 = bf16[32,1,16,1024]{3,2,1,0:T(8,128)(2,1)S(1)} async-done(((bf16[32,1,16,1024]{3,2,1,0:T(8,128)(2,1)}), bf16[32,1,16,1024]{3,2,1,0:T(8,128)(2,1)S(1)}, u32[]{:S(2)}, u32[]{:S(2)}) %all-to-all-start.3) | async-done | bytes 1048608 | tf_op jit(solution)/shard_map/all_to_all | solution.py:93
  180.3 22.1 %reduce-scatter.4.cloned.1.call-done = bf16[64,1536]{1,0:T(8,128)(2,1)} async-done(((bf16[1024,1536]{1,0:T(8,128)(2,1)}), bf16[64,1536]{1,0:T(8,128)(2,1)}) %reduce-scatter.4.cloned.1.call-update) | async-done | bytes 196624
  204.4 140.6 %all-reduce.2.cloned.1.call-done = bf16[1,768,1024]{2,1,0:T(8,128)(2,1)} async-done(((bf16[1,768,1024]{2,1,0:T(8,128)(2,1)}), bf16[1,768,1024]{2,1,0:T(8,128)(2,1)}) %all-reduce.2.cloned.1.call-update) | async-done | bytes 1572880 | tf_op jit(solution)/shard_map/psum | solution.py:114
  345.0 2.7 copy.132
  (79 shorter events, 20.8 us)
Async XLA Ops:
  7.2 14.9 %copy-start = (bf16[128,1024]{1,0:T(8,128)(2,1)S(1)}, bf16[128,1024]{1,0:T(8,128)(2,1)}, u32[]{:S(2)}) copy-start(bf16[128,1024]{1,0:T(8,128)(2,1)} %param.9) | copy-start | bytes 786436
  7.2 83.8 %all-gather.2.cloned.1.call-start = ((), (), s32[]{:S(2)}) async-start(), calls=%async_computation.6 | async-start | bytes 3342336 | tf_op jit(solution)/shard_map/all_gather | solution.py:76
  10.8 11.0 %copy-start.6 = (s32[128,2]{0,1:T(2,128)}, s32[128,2]{0,1:T(2,128)S(1)}, u32[]{:S(2)}) copy-start(s32[128,2]{0,1:T(2,128)S(1)} %multiply_add_fusion) | copy-start | bytes 3076
  12.5 15.6 %all-to-all-start = ((bf16[32,1,16]{2,1,0:T(2,128)(2,1)}), bf16[32,1,16]{2,1,0:T(2,128)(2,1)S(1)}, u32[]{:S(2)}, u32[]{:S(2)}) async-start(bf16[32,1,16]{2,1,0:T(2,128)(2,1)} %reshape.263), calls=%async_computation | async-start | bytes 32768 | tf_op jit(solution)/shard_map/all_to_all | solution.py:70
  22.0 11.8 %copy-start.9 = (s32[8,1,2]{0,2,1:T(2,128)S(1)}, s32[8,1,2]{0,2,1:T(2,128)}, u32[]{:S(2)}) copy-start(s32[8,1,2]{0,2,1:T(2,128)} %param.15) | copy-start | bytes 196
  22.0 11.8 %copy-start.10 = (f32[16]{0:T(128)S(1)}, f32[16]{0:T(128)}, u32[]{:S(2)}) copy-start(f32[16]{0:T(128)} %param.17) | copy-start | bytes 196
  22.0 12.0 %copy-start.13 = (s32[1,6]{1,0:T(1,128)S(1)}, s32[1,6]{1,0:T(1,128)}, u32[]{:S(2)}) copy-start(s32[1,6]{1,0:T(1,128)} %param.16) | copy-start | bytes 76
  22.0 12.9 %copy-start.4 = (bf16[128,1024]{1,0:T(8,128)(2,1)S(1)}, bf16[128,1024]{1,0:T(8,128)(2,1)}, u32[]{:S(2)}) copy-start(bf16[128,1024]{1,0:T(8,128)(2,1)} %param.10) | copy-start | bytes 786436
  28.0 66.2 %all-to-all-start.2 = ((bf16[32,1,16,1024]{3,2,1,0:T(8,128)(2,1)}), bf16[32,1,16,1024]{3,2,1,0:T(8,128)(2,1)}, u32[]{:S(2)}, u32[]{:S(2)}) async-start(bf16[32,1,16,1024]{3,2,1,0:T(8,128)(2,1)} %bitcast.20), calls=%async_computation.2 | async-start | bytes 2097152 | tf_op jit(solution)/shard_map/all_to_all | solution.py:68
  94.2 23.6 %all-to-all-start.1 = ((bf16[32,1,16,1024]{3,2,1,0:T(8,128)(2,1)}), bf16[32,1,16,1024]{3,2,1,0:T(8,128)(2,1)}, u32[]{:S(2)}, u32[]{:S(2)}) async-start(bf16[32,1,16,1024]{3,2,1,0:T(8,128)(2,1)} %bitcast.158), calls=%async_computation.1 | async-start | bytes 2097152 | tf_op jit(solution)/shard_map/all_to_all | solution.py:69
  101.7 100.8 %reduce-scatter.4.cloned.1.call-start = ((), (), s32[]{:S(2)}) async-start(), calls=%async_computation.8 | async-start | bytes 3342336
  102.7 2.9 copy-start.1
  107.3 10.6 %copy-start.8 = (f32[768]{0:T(1024)S(1)}, f32[768]{0:T(1024)}, u32[]{:S(2)}) copy-start(f32[768]{0:T(1024)} %broadcast_bitcast_fusion.1) | copy-start | bytes 9220
  107.3 10.6 %copy-start.11 = (bf16[1,768,1024]{2,1,0:T(8,128)(2,1)S(1)}, bf16[1,768,1024]{2,1,0:T(8,128)(2,1)}, u32[]{:S(2)}) copy-start(bf16[1,768,1024]{2,1,0:T(8,128)(2,1)} %param.14) | copy-start | bytes 4718596
  117.8 9.2 %slice-start = ((s8[6291456]{0:T(1024)(128)(4,1)}), s8[4194304]{0:T(1024)(128)(4,1)S(1)}, s32[]{:S(2)}) async-start(s8[6291456]{0:T(1024)(128)(4,1)} %bitcast.155), calls=%async_computation.9 | async-start | bytes 8388608
  123.1 3.8 %copy-start.15 = (bf16[32,16,768]{2,0,1:T(8,128)(2,1)}, bf16[32,16,768]{2,0,1:T(8,128)(2,1)S(1)}, u32[]{:S(2)}) copy-start(bf16[32,16,768]{2,0,1:T(8,128)(2,1)S(1)} %get-tuple-element.24) | copy-start | bytes 2359300
  123.1 3.8 %copy-start.16 = (bf16[32,16,768]{2,0,1:T(8,128)(2,1)}, bf16[32,16,768]{2,0,1:T(8,128)(2,1)S(1)}, u32[]{:S(2)}) copy-start(bf16[32,16,768]{2,0,1:T(8,128)(2,1)S(1)} %get-tuple-element.25) | copy-start | bytes 2359300
  123.1 3.9 %slice-start.1 = ((s8[6291456]{0:T(1024)(128)(4,1)}), s8[2097152]{0:T(1024)(128)(4,1)S(1)}, s32[]{:S(2)}) async-start(s8[6291456]{0:T(1024)(128)(4,1)} %bitcast.155), calls=%async_computation.10 | async-start | bytes 4194304
  136.0 22.0 %all-to-all-start.4 = ((bf16[32,1,16,1024]{3,2,1,0:T(8,128)(2,1)}), bf16[32,1,16,1024]{3,2,1,0:T(8,128)(2,1)}, u32[]{:S(2)}, u32[]{:S(2)}) async-start(bf16[32,1,16,1024]{3,2,1,0:T(8,128)(2,1)} %copy.94), calls=%async_computation.4 | async-start | bytes 2097152 | tf_op jit(solution)/shard_map/all_to_all | solution.py:98
  141.8 4.4 %copy-start.3 = (bf16[1024,1536,1]{0,1,2:T(8,128)(2,1)S(1)}, bf16[1024,1536,1]{0,1,2:T(8,128)(2,1)}, u32[]{:S(2)}) copy-start(bf16[1024,1536,1]{0,1,2:T(8,128)(2,1)} %copy-done.2) | copy-start | bytes 9437188
  141.8 203.2 %all-reduce.2.cloned.1.call-start = ((), (), s32[]{:S(2)}) async-start(), calls=%async_computation.7 | async-start | bytes 3145728 | tf_op jit(solution)/shard_map/psum | solution.py:114
  149.3 13.7 %copy-start.5 = (bf16[128,1024]{1,0:T(8,128)(2,1)S(1)}, bf16[128,1024]{1,0:T(8,128)(2,1)}, u32[]{:S(2)}) copy-start(bf16[128,1024]{1,0:T(8,128)(2,1)} %param.10) | copy-start | bytes 786436
  149.3 13.8 %copy-start.7 = (s32[128,2]{0,1:T(2,128)S(1)}, s32[128,2]{0,1:T(2,128)}, u32[]{:S(2)}) copy-start(s32[128,2]{0,1:T(2,128)} %copy-done.6) | copy-start | bytes 3076
  158.0 21.3 %all-to-all-start.3 = ((bf16[32,1,16,1024]{3,2,1,0:T(8,128)(2,1)}), bf16[32,1,16,1024]{3,2,1,0:T(8,128)(2,1)S(1)}, u32[]{:S(2)}, u32[]{:S(2)}) async-start(bf16[32,1,16,1024]{3,2,1,0:T(8,128)(2,1)} %copy.93), calls=%async_computation.3 | async-start | bytes 2097152 | tf_op jit(solution)/shard_map/all_to_all | solution.py:93
  (3 other events, 4.7 us)
Sparse Core Ops, SparseCore 0:
  10.1 80.8 all-gather.1
  131.9 70.4 reduce-scatter.3
  205.3 139.6 all-reduce.1
where the time goes:
time: 355 us; the launch traced here: 354 us
  waiting for transfers between devices  249 us (70%)
  starting transfers between devices  33.8 us (10%)
  matrix products  29.7 us (8%)
  local copies, waits for them, and re-layouts  22.7 us (6%)
  between operations  14.1 us (4%)
  other arithmetic  4.95 us (1%)
    psum x1, waiting for transfers between devices, body(): down_grad = lax.psum(down_part.astype(jnp.bfloat16), 'dp')  141 us
    all_gather x1, waiting for transfers between devices, body(): gathered = lax.all_gather(gate_up_weight, 'dp', axis=0, tiled=True)  54.6 us
    unnamed x4, waiting for transfers between devices  22.8 us
    all_to_all x1, waiting for transfers between devices, body(): lax.all_to_all(row_grads, 'expert', split_axis=0, concat_axis=0, tiled=True)  13.8 us
    unnamed x45, local copies, waits for them, and re-layouts  13.5 us
    all_to_all x1, starting transfers between devices, body(): lax.all_to_all(send_probs, 'expert', split_axis=0, concat_axis=0, tiled=T...  9.4 us
    all_to_all x1, starting transfers between devices, body(): lax.all_to_all(send_grads, 'expert', split_axis=0, concat_axis=0, tiled=T...  7.43 us
  transfers between devices with their start and end apart: 8, of which 7 were waited for; matrix products, arithmetic and copies ran while one was open for 10% of the time, Pallas kernels for 0%

commit v1 on v0

--- a/solution.py
+++ b/solution.py
@@ -73,7 +73,16 @@
     full_scale = jnp.repeat(level_rows, hidden, axis=2)
     down_scale = jnp.repeat(lookup(down_scale_index, scale_table), QBLOCK, axis=1)
     down_eff = (down_weight.astype(f32) * down_scale[:, :, None]).astype(jnp.bfloat16)
-    gathered = lax.all_gather(gate_up_weight, "dp", axis=0, tiled=True)
+    ways = lax.axis_size("dp")
+    up = [(d, (d + 1) % ways) for d in range(ways)]
+    down = [(d, (d - 1) % ways) for d in range(ways)]
+    earlier, later = ([gate_up_weight], [gate_up_weight])
+    for _ in range(ways // 2):
+        earlier.append(lax.ppermute(earlier[-1], "dp", up))
+    for _ in range((ways - 1) // 2):
+        later.append(lax.ppermute(later[-1], "dp", down))
+    line = jnp.concatenate([*earlier[::-1], *later[1:]], axis=0)
+    gathered = jnp.roll(line, (lax.axis_index("dp") - ways // 2) * gate_up_weight.shape[0], axis=0)
     gate_up_eff = (gathered.astype(f32) * full_scale).astype(jnp.bfloat16)
     projected = jnp.einsum("sjcd,djf->sjcf", recv_tokens, gate_up_eff, preferred_element_type=f32)
     gate_part = projected[..., :hidden]

time: 355 us -> 412 us (1.16)
  starting transfers between devices: 33.8 us -> 93.1 us
  waiting for transfers between devices: 249 us -> 219 us
  local copies, waits for them, and re-layouts: 22.7 us -> 42.2 us
    ppermute x0 -> x15, starting transfers between devices: none -> 59.4 us  [the longest x7 42.1 us: body(): later.append(lax.ppermute(later[-1], 'dp', down))]
    all_gather x1 -> x0, waiting for transfers between devices: 54.6 us -> none  [body(): gathered = lax.all_gather(gate_up_weight, 'dp', axis=0, tiled=True)]
    ppermute x0 -> x15, waiting for transfers between devices: none -> 33.3 us  [the longest x7 23.7 us: body(): later.append(lax.ppermute(later[-1], 'dp', down))]
    concatenate x0 -> x1, local copies, waits for them, and re-layouts: none -> 16.5 us  [body(): jnp.roll(line, (lax.axis_index('dp') - ways // 2) * gate_up_weight.shape[...]
    unnamed x45 -> x42, local copies, waits for them, and re-layouts: 13.5 us -> 19 us
    all_to_all x1, waiting for transfers between devices: 4.52 us -> 0.01 us  [body(): lax.all_to_all(send_probs, 'expert', split_axis=0, concat_axis=0, tiled=T...]
    unnamed x4 -> x3, waiting for transfers between devices: 22.8 us -> 23.2 us
  transfers between devices with their start and end apart: 8 -> 22, of which waited for: 7 -> 12; matrix products, arithmetic and copies ran while one was open for 10% -> 14% of each run, Pallas kernels for 0% -> 0%
where the time goes in v1:
time: 412 us; the launch traced here: 409 us
  waiting for transfers between devices  219 us (53%)
  starting transfers between devices  93.1 us (23%)
  local copies, waits for them, and re-layouts  42.2 us (10%)
  matrix products  31.9 us (8%)
  between operations  14.6 us (4%)
  other arithmetic  7.89 us (2%)
    psum x1, waiting for transfers between devices, body(): down_grad = lax.psum(down_part.astype(jnp.bfloat16), 'dp')  140 us
    ppermute x7, starting transfers between devices, body(): later.append(lax.ppermute(later[-1], 'dp', down))  42.1 us
    ppermute x7, waiting for transfers between devices, body(): later.append(lax.ppermute(later[-1], 'dp', down))  23.7 us
    unnamed x3, waiting for transfers between devices  23.2 us
    unnamed x42, local copies, waits for them, and re-layouts  19 us
    ppermute x8, starting transfers between devices, body(): earlier.append(lax.ppermute(earlier[-1], 'dp', up))  17.3 us
    concatenate x1, local copies, waits for them, and re-layouts, body(): jnp.roll(line, (lax.axis_index('dp') - ways // 2) * gate_up_weight.shape[...  16.5 us
    all_to_all x1, waiting for transfers between devices, body(): lax.all_to_all(row_grads, 'expert', split_axis=0, concat_axis=0, tiled=True)  13.8 us
  transfers between devices with their start and end apart: 22, of which 12 were waited for; matrix products, arithmetic and copies ran while one was open for 14% of the time, Pallas kernels for 0%

profile of v1, /device:TPU:2, one launch (start us, length us, event | category | flops | bytes accessed | tf_op | source)
XLA Modules:
  0.0 409.1 jit_solution(17823563916355118716)
XLA Ops:
  12.2 9.5 %collective-permute-start.8 = (bf16[64,1,1536]{0,2,1:T(8,128)(2,1)S(1)}, bf16[64,1,1536]{0,2,1:T(8,128)(2,1)S(1)}, u32[]{:S(2)}, u32[]{:S(2)}) collective-permute-start(bf16[64,1,1536]{0,2,1:T(8,128)(2,1)S(1)} %copy.96), channel_id=1, source_target_pairs={{0,480},{32,0},{64,32},{96,64},{128,96},{160,128},{192,160},{224,1... | collective-permute-start | bytes 589832 | tf_op jit(solution)/shard_map/ppermute | solution.py:83
  24.6 4.2 %collective-permute-done = bf16[64,1,1536]{0,2,1:T(8,128)(2,1)S(1)} collective-permute-done((bf16[64,1,1536]{0,2,1:T(8,128)(2,1)S(1)}, bf16[64,1,1536]{0,2,1:T(8,128)(2,1)S(1)}, u32[]{:S(2)}, u32[]{:S(2)}) %collective-permute-start) | collective-permute-done | bytes 196640 | tf_op jit(solution)/shard_map/ppermute | solution.py:81
  32.4 7.6 %all-to-all-start = ((bf16[32,1,16]{2,1,0:T(2,128)(2,1)}), bf16[32,1,16]{2,1,0:T(2,128)(2,1)S(1)}, u32[]{:S(2)}, u32[]{:S(2)}) async-start(bf16[32,1,16]{2,1,0:T(2,128)(2,1)} %reshape.263), calls=%async_computation | async-start | bytes 32768 | tf_op jit(solution)/shard_map/all_to_all | solution.py:70
  40.1 5.1 %collective-permute-start.9 = (bf16[64,1,1536]{0,2,1:T(8,128)(2,1)S(1)}, bf16[64,1,1536]{0,2,1:T(8,128)(2,1)S(1)}, u32[]{:S(2)}, u32[]{:S(2)}) collective-permute-start(bf16[64,1,1536]{0,2,1:T(8,128)(2,1)S(1)} %collective-permute-done.8), channel_id=1, source_target_pairs={{0,480},{32,0},{64,32},{96,64},{128,96},{160,128},{192,160},{224,1... | collective-permute-start | bytes 589832 | tf_op jit(solution)/shard_map/ppermute | solution.py:83
  47.3 6.6 %collective-permute-done.9 = bf16[64,1,1536]{0,2,1:T(8,128)(2,1)S(1)} collective-permute-done((bf16[64,1,1536]{0,2,1:T(8,128)(2,1)S(1)}, bf16[64,1,1536]{0,2,1:T(8,128)(2,1)S(1)}, u32[]{:S(2)}, u32[]{:S(2)}) %collective-permute-start.9) | collective-permute-done | bytes 196640 | tf_op jit(solution)/shard_map/ppermute | solution.py:83
  53.9 5.6 %collective-permute-start.10 = (bf16[64,1,1536]{0,2,1:T(8,128)(2,1)S(1)}, bf16[64,1,1536]{0,2,1:T(8,128)(2,1)S(1)}, u32[]{:S(2)}, u32[]{:S(2)}) collective-permute-start(bf16[64,1,1536]{0,2,1:T(8,128)(2,1)S(1)} %collective-permute-done.9), channel_id=1, source_target_pairs={{0,480},{32,0},{64,32},{96,64},{128,96},{160,128},{192,160},{224,1... | collective-permute-start | bytes 589832 | tf_op jit(solution)/shard_map/ppermute | solution.py:83
  61.5 5.9 %collective-permute-done.10 = bf16[64,1,1536]{0,2,1:T(8,128)(2,1)S(1)} collective-permute-done((bf16[64,1,1536]{0,2,1:T(8,128)(2,1)S(1)}, bf16[64,1,1536]{0,2,1:T(8,128)(2,1)S(1)}, u32[]{:S(2)}, u32[]{:S(2)}) %collective-permute-start.10) | collective-permute-done | bytes 196640 | tf_op jit(solution)/shard_map/ppermute | solution.py:83
  67.3 5.6 %collective-permute-start.11 = (bf16[64,1,1536]{0,2,1:T(8,128)(2,1)S(1)}, bf16[64,1,1536]{0,2,1:T(8,128)(2,1)}, u32[]{:S(2)}, u32[]{:S(2)}) collective-permute-start(bf16[64,1,1536]{0,2,1:T(8,128)(2,1)S(1)} %collective-permute-done.10), channel_id=1, source_target_pairs={{0,480},{32,0},{64,32},{96,64},{128,96},{160,128},{192,160},{224,1... | collective-permute-start | bytes 589832 | tf_op jit(solution)/shard_map/ppermute | solution.py:83
  76.3 7.4 %all-to-all-start.2 = ((bf16[32,1,16,1024]{3,2,1,0:T(8,128)(2,1)}), bf16[32,1,16,1024]{3,2,1,0:T(8,128)(2,1)}, u32[]{:S(2)}, u32[]{:S(2)}) async-start(bf16[32,1,16,1024]{3,2,1,0:T(8,128)(2,1)} %bitcast.20), calls=%async_computation.2 | async-start | bytes 2097152 | tf_op jit(solution)/shard_map/all_to_all | solution.py:68
  84.6 5.1 %collective-permute-start.12 = (bf16[64,1,1536]{0,2,1:T(8,128)(2,1)}, bf16[64,1,1536]{0,2,1:T(8,128)(2,1)}, u32[]{:S(2)}, u32[]{:S(2)}) collective-permute-start(bf16[64,1,1536]{0,2,1:T(8,128)(2,1)} %collective-permute-done.11), channel_id=1, source_target_pairs={{0,480},{32,0},{64,32},{96,64},{128,96},{160,128},{192,160},{224,1... | collective-permute-start | bytes 589832 | tf_op jit(solution)/shard_map/ppermute | solution.py:83
  98.7 5.6 %collective-permute-start.13 = (bf16[64,1,1536]{0,2,1:T(8,128)(2,1)}, bf16[64,1,1536]{0,2,1:T(8,128)(2,1)}, u32[]{:S(2)}, u32[]{:S(2)}) collective-permute-start(bf16[64,1,1536]{0,2,1:T(8,128)(2,1)} %collective-permute-done.12), channel_id=1, source_target_pairs={{0,480},{32,0},{64,32},{96,64},{128,96},{160,128},{192,160},{224,1... | collective-permute-start | bytes 589832 | tf_op jit(solution)/shard_map/ppermute | solution.py:83
  112.4 5.6 %collective-permute-start.14 = (bf16[64,1,1536]{0,2,1:T(8,128)(2,1)}, bf16[64,1,1536]{0,2,1:T(8,128)(2,1)}, u32[]{:S(2)}, u32[]{:S(2)}) collective-permute-start(bf16[64,1,1536]{0,2,1:T(8,128)(2,1)} %collective-permute-done.13), channel_id=1, source_target_pairs={{0,480},{32,0},{64,32},{96,64},{128,96},{160,128},{192,160},{224,1... | collective-permute-start | bytes 589832 | tf_op jit(solution)/shard_map/ppermute | solution.py:83
  125.3 5.3 %collective-permute-done.7 = bf16[64,1,1536]{0,2,1:T(8,128)(2,1)} collective-permute-done((bf16[64,1,1536]{0,2,1:T(8,128)(2,1)}, bf16[64,1,1536]{0,2,1:T(8,128)(2,1)}, u32[]{:S(2)}, u32[]{:S(2)}) %collective-permute-start.7) | collective-permute-done | bytes 196640 | tf_op jit(solution)/shard_map/ppermute | solution.py:81
  130.6 16.5 %concatenate.18 = bf16[2048,1,1536]{0,2,1:T(8,128)(2,1)} concatenate(bf16[64,1,1536]{0,2,1:T(8,128)(2,1)} %collective-permute-done.7, bf16[64,1,1536]{0,2,1:T(8,128)(2,1)} %collective-permute-done.6, bf16[64,1,1536]{0,2,1:T(8,128)(2,1)} %collective-permute-done.5, bf16[64,1,1536]{0,2,1:T(8,128)(2,1)} %collective-permute-done.4, bf16[64,1,1536]{0,2,1:T(8,128)(2,1)S(1)} %collective-permute-done.3, ...), dimensions={0} | concatenate | bytes 12582912 | tf_op jit(solution)/shard_map/jit(_roll_dynamic)/concatenate | solution.py:85
  147.2 7.4 %all-to-all-start.1 = ((bf16[32,1,16,1024]{3,2,1,0:T(8,128)(2,1)}), bf16[32,1,16,1024]{3,2,1,0:T(8,128)(2,1)S(1)}, u32[]{:S(2)}, u32[]{:S(2)}) async-start(bf16[32,1,16,1024]{3,2,1,0:T(8,128)(2,1)} %bitcast.14), calls=%async_computation.1 | async-start | bytes 2097152 | tf_op jit(solution)/shard_map/all_to_all | solution.py:69
  155.6 4.2 %copy-done.2 = bf16[2048,1,1536]{0,2,1:T(8,128)(2,1)S(1)} copy-done((bf16[2048,1,1536]{0,2,1:T(8,128)(2,1)S(1)}, bf16[2048,1,1536]{0,2,1:T(8,128)(2,1)}, u32[]{:S(2)}) %copy-start.2) | copy-done | bytes 6291480
  163.8 5.3 %convolution_bitcast_fusion = f32[32,1,16,1536]{3,0,2,1:T(8,128)} fusion(bf16[1024,1536,1]{0,1,2:T(8,128)(2,1)S(1)} %fusion.3, bf16[32,1,16,1024]{3,2,1,0:T(8,128)(2,1)} %all-to-all-done.2), kind=kOutput, calls=%fused_computation.4 | convolution fusion | flops 1610612736 | bytes 7340032 | tf_op jit(solution)/shard_map/sjcd,djf->sjcf/dot_general | solution.py:87
  170.7 5.3 %fusion.29 = (bf16[32,16,768]{2,0,1:T(8,128)(2,1)S(1)}, bf16[32,16,768]{2,0,1:T(8,128)(2,1)S(1)}, bf16[32,1,16,768]{3,0,2,1:T(8,128)(2,1)}) fusion(f32[32,1,16,1536]{3,0,2,1:T(8,128)} %convolution_bitcast_fusion, bf16[32,1,16,1024]{3,2,1,0:T(8,128)(2,1)S(1)} %all-to-all-done.1, bf16[1,768,1024]{2,1,0:T(8,128)(2,1)S(1)} %copy-done.11, ...), kind=kOutput, calls=%fused_computation.46 | convolution fusion | flops 813957120 | bytes 8131584 | tf_op jit(solution)/shard_map/sjcd,jfd->sjcf/dot_general | solution.py:93
  189.8 5.8 %all-to-all-start.4 = ((bf16[32,1,16,1024]{3,2,1,0:T(8,128)(2,1)}), bf16[32,1,16,1024]{3,2,1,0:T(8,128)(2,1)}, u32[]{:S(2)}, u32[]{:S(2)}) async-start(bf16[32,1,16,1024]{3,2,1,0:T(8,128)(2,1)} %copy.109), calls=%async_computation.4 | async-start | bytes 2097152 | tf_op jit(solution)/shard_map/all_to_all | solution.py:107
  204.7 7.1 %all-to-all-done.4 = bf16[32,1,16,1024]{3,2,1,0:T(8,128)(2,1)} async-done(((bf16[32,1,16,1024]{3,2,1,0:T(8,128)(2,1)}), bf16[32,1,16,1024]{3,2,1,0:T(8,128)(2,1)}, u32[]{:S(2)}, u32[]{:S(2)}) %all-to-all-start.4) | async-done | bytes 1048608 | tf_op jit(solution)/shard_map/all_to_all | solution.py:107
  211.8 5.0 %all-to-all-start.3 = ((bf16[32,1,16,1024]{3,2,1,0:T(8,128)(2,1)}), bf16[32,1,16,1024]{3,2,1,0:T(8,128)(2,1)S(1)}, u32[]{:S(2)}, u32[]{:S(2)}) async-start(bf16[32,1,16,1024]{3,2,1,0:T(8,128)(2,1)} %copy.108), calls=%async_computation.3 | async-start | bytes 2097152 | tf_op jit(solution)/shard_map/all_to_all | solution.py:102
  219.3 13.8 %all-to-all-done.3 = bf16[32,1,16,1024]{3,2,1,0:T(8,128)(2,1)S(1)} async-done(((bf16[32,1,16,1024]{3,2,1,0:T(8,128)(2,1)}), bf16[32,1,16,1024]{3,2,1,0:T(8,128)(2,1)S(1)}, u32[]{:S(2)}, u32[]{:S(2)}) %all-to-all-start.3) | async-done | bytes 1048608 | tf_op jit(solution)/shard_map/all_to_all | solution.py:102
  234.1 23.1 %reduce-scatter.4.cloned.1.call-done = bf16[64,1536]{1,0:T(8,128)(2,1)} async-done(((bf16[1024,1536]{1,0:T(8,128)(2,1)}), bf16[64,1536]{1,0:T(8,128)(2,1)}) %reduce-scatter.4.cloned.1.call-update) | async-done | bytes 196624
  259.2 140.3 %all-reduce.2.cloned.1.call-done = bf16[1,768,1024]{2,1,0:T(8,128)(2,1)} async-done(((bf16[1,768,1024]{2,1,0:T(8,128)(2,1)}), bf16[1,768,1024]{2,1,0:T(8,128)(2,1)}) %all-reduce.2.cloned.1.call-update) | async-done | bytes 1572880 | tf_op jit(solution)/shard_map/psum | solution.py:123
  (103 shorter events, 81.4 us)
Async XLA Ops:
  7.2 67.7 %copy-start = (bf16[128,1024]{1,0:T(8,128)(2,1)S(1)}, bf16[128,1024]{1,0:T(8,128)(2,1)}, u32[]{:S(2)}) copy-start(bf16[128,1024]{1,0:T(8,128)(2,1)} %param.9) | copy-start | bytes 786436
  8.4 20.5 %collective-permute-start = (bf16[64,1,1536]{0,2,1:T(8,128)(2,1)S(1)}, bf16[64,1,1536]{0,2,1:T(8,128)(2,1)S(1)}, u32[]{:S(2)}, u32[]{:S(2)}) collective-permute-start(bf16[64,1,1536]{0,2,1:T(8,128)(2,1)S(1)} %copy.96), channel_id=1, source_target_pairs={{0,32},{32,64},{64,96},{96,128},{128,160},{160,192},{192,224},{224... | collective-permute-start | bytes 589832 | tf_op jit(solution)/shard_map/ppermute | solution.py:81
  12.2 27.8 %collective-permute-start.8 = (bf16[64,1,1536]{0,2,1:T(8,128)(2,1)S(1)}, bf16[64,1,1536]{0,2,1:T(8,128)(2,1)S(1)}, u32[]{:S(2)}, u32[]{:S(2)}) collective-permute-start(bf16[64,1,1536]{0,2,1:T(8,128)(2,1)S(1)} %copy.96), channel_id=1, source_target_pairs={{0,480},{32,0},{64,32},{96,64},{128,96},{160,128},{192,160},{224,1... | collective-permute-start | bytes 589832 | tf_op jit(solution)/shard_map/ppermute | solution.py:83
  24.6 22.6 %copy-start.8 = (s32[128,2]{0,1:T(2,128)}, s32[128,2]{0,1:T(2,128)S(1)}, u32[]{:S(2)}) copy-start(s32[128,2]{0,1:T(2,128)S(1)} %multiply_add_fusion) | copy-start | bytes 3076
  28.9 16.3 %collective-permute-start.1 = (bf16[64,1,1536]{0,2,1:T(8,128)(2,1)S(1)}, bf16[64,1,1536]{0,2,1:T(8,128)(2,1)S(1)}, u32[]{:S(2)}, u32[]{:S(2)}) collective-permute-start(bf16[64,1,1536]{0,2,1:T(8,128)(2,1)S(1)} %collective-permute-done), channel_id=1, source_target_pairs={{0,32},{32,64},{64,96},{96,128},{128,160},{160,192},{192,224},{224... | collective-permute-start | bytes 589832 | tf_op jit(solution)/shard_map/ppermute | solution.py:81
  32.4 43.9 %all-to-all-start = ((bf16[32,1,16]{2,1,0:T(2,128)(2,1)}), bf16[32,1,16]{2,1,0:T(2,128)(2,1)S(1)}, u32[]{:S(2)}, u32[]{:S(2)}) async-start(bf16[32,1,16]{2,1,0:T(2,128)(2,1)} %reshape.263), calls=%async_computation | async-start | bytes 32768 | tf_op jit(solution)/shard_map/all_to_all | solution.py:70
  40.1 13.8 %collective-permute-start.9 = (bf16[64,1,1536]{0,2,1:T(8,128)(2,1)S(1)}, bf16[64,1,1536]{0,2,1:T(8,128)(2,1)S(1)}, u32[]{:S(2)}, u32[]{:S(2)}) collective-permute-start(bf16[64,1,1536]{0,2,1:T(8,128)(2,1)S(1)} %collective-permute-done.8), channel_id=1, source_target_pairs={{0,480},{32,0},{64,32},{96,64},{128,96},{160,128},{192,160},{224,1... | collective-permute-start | bytes 589832 | tf_op jit(solution)/shard_map/ppermute | solution.py:83
  45.2 14.3 %collective-permute-start.2 = (bf16[64,1,1536]{0,2,1:T(8,128)(2,1)S(1)}, bf16[64,1,1536]{0,2,1:T(8,128)(2,1)S(1)}, u32[]{:S(2)}, u32[]{:S(2)}) collective-permute-start(bf16[64,1,1536]{0,2,1:T(8,128)(2,1)S(1)} %collective-permute-done.1), channel_id=1, source_target_pairs={{0,32},{32,64},{64,96},{96,128},{128,160},{160,192},{192,224},{224... | collective-permute-start | bytes 589832 | tf_op jit(solution)/shard_map/ppermute | solution.py:81
  53.9 13.4 %collective-permute-start.10 = (bf16[64,1,1536]{0,2,1:T(8,128)(2,1)S(1)}, bf16[64,1,1536]{0,2,1:T(8,128)(2,1)S(1)}, u32[]{:S(2)}, u32[]{:S(2)}) collective-permute-start(bf16[64,1,1536]{0,2,1:T(8,128)(2,1)S(1)} %collective-permute-done.9), channel_id=1, source_target_pairs={{0,480},{32,0},{64,32},{96,64},{128,96},{160,128},{192,160},{224,1... | collective-permute-start | bytes 589832 | tf_op jit(solution)/shard_map/ppermute | solution.py:83
  59.5 13.4 %collective-permute-start.3 = (bf16[64,1,1536]{0,2,1:T(8,128)(2,1)S(1)}, bf16[64,1,1536]{0,2,1:T(8,128)(2,1)S(1)}, u32[]{:S(2)}, u32[]{:S(2)}) collective-permute-start(bf16[64,1,1536]{0,2,1:T(8,128)(2,1)S(1)} %collective-permute-done.2), channel_id=1, source_target_pairs={{0,32},{32,64},{64,96},{96,128},{128,160},{160,192},{192,224},{224... | collective-permute-start | bytes 589832 | tf_op jit(solution)/shard_map/ppermute | solution.py:81
  67.3 17.3 %collective-permute-start.11 = (bf16[64,1,1536]{0,2,1:T(8,128)(2,1)S(1)}, bf16[64,1,1536]{0,2,1:T(8,128)(2,1)}, u32[]{:S(2)}, u32[]{:S(2)}) collective-permute-start(bf16[64,1,1536]{0,2,1:T(8,128)(2,1)S(1)} %collective-permute-done.10), channel_id=1, source_target_pairs={{0,480},{32,0},{64,32},{96,64},{128,96},{160,128},{192,160},{224,1... | collective-permute-start | bytes 589832 | tf_op jit(solution)/shard_map/ppermute | solution.py:83
  72.9 16.8 %collective-permute-start.4 = (bf16[64,1,1536]{0,2,1:T(8,128)(2,1)S(1)}, bf16[64,1,1536]{0,2,1:T(8,128)(2,1)}, u32[]{:S(2)}, u32[]{:S(2)}) collective-permute-start(bf16[64,1,1536]{0,2,1:T(8,128)(2,1)S(1)} %collective-permute-done.3), channel_id=1, source_target_pairs={{0,32},{32,64},{64,96},{96,128},{128,160},{160,192},{192,224},{224... | collective-permute-start | bytes 589832 | tf_op jit(solution)/shard_map/ppermute | solution.py:81
  76.3 70.9 %all-to-all-start.2 = ((bf16[32,1,16,1024]{3,2,1,0:T(8,128)(2,1)}), bf16[32,1,16,1024]{3,2,1,0:T(8,128)(2,1)}, u32[]{:S(2)}, u32[]{:S(2)}) async-start(bf16[32,1,16,1024]{3,2,1,0:T(8,128)(2,1)} %bitcast.20), calls=%async_computation.2 | async-start | bytes 2097152 | tf_op jit(solution)/shard_map/all_to_all | solution.py:68
  84.6 14.1 %collective-permute-start.12 = (bf16[64,1,1536]{0,2,1:T(8,128)(2,1)}, bf16[64,1,1536]{0,2,1:T(8,128)(2,1)}, u32[]{:S(2)}, u32[]{:S(2)}) collective-permute-start(bf16[64,1,1536]{0,2,1:T(8,128)(2,1)} %collective-permute-done.11), channel_id=1, source_target_pairs={{0,480},{32,0},{64,32},{96,64},{128,96},{160,128},{192,160},{224,1... | collective-permute-start | bytes 589832 | tf_op jit(solution)/shard_map/ppermute | solution.py:83
  89.7 14.6 %collective-permute-start.5 = (bf16[64,1,1536]{0,2,1:T(8,128)(2,1)}, bf16[64,1,1536]{0,2,1:T(8,128)(2,1)}, u32[]{:S(2)}, u32[]{:S(2)}) collective-permute-start(bf16[64,1,1536]{0,2,1:T(8,128)(2,1)} %collective-permute-done.4), channel_id=1, source_target_pairs={{0,32},{32,64},{64,96},{96,128},{128,160},{160,192},{192,224},{224... | collective-permute-start | bytes 589832 | tf_op jit(solution)/shard_map/ppermute | solution.py:81
  98.7 13.7 %collective-permute-start.13 = (bf16[64,1,1536]{0,2,1:T(8,128)(2,1)}, bf16[64,1,1536]{0,2,1:T(8,128)(2,1)}, u32[]{:S(2)}, u32[]{:S(2)}) collective-permute-start(bf16[64,1,1536]{0,2,1:T(8,128)(2,1)} %collective-permute-done.12), channel_id=1, source_target_pairs={{0,480},{32,0},{64,32},{96,64},{128,96},{160,128},{192,160},{224,1... | collective-permute-start | bytes 589832 | tf_op jit(solution)/shard_map/ppermute | solution.py:83
  104.3 13.7 %collective-permute-start.6 = (bf16[64,1,1536]{0,2,1:T(8,128)(2,1)}, bf16[64,1,1536]{0,2,1:T(8,128)(2,1)}, u32[]{:S(2)}, u32[]{:S(2)}) collective-permute-start(bf16[64,1,1536]{0,2,1:T(8,128)(2,1)} %collective-permute-done.5), channel_id=1, source_target_pairs={{0,32},{32,64},{64,96},{96,128},{128,160},{160,192},{192,224},{224... | collective-permute-start | bytes 589832 | tf_op jit(solution)/shard_map/ppermute | solution.py:81
  112.4 12.8 %collective-permute-start.14 = (bf16[64,1,1536]{0,2,1:T(8,128)(2,1)}, bf16[64,1,1536]{0,2,1:T(8,128)(2,1)}, u32[]{:S(2)}, u32[]{:S(2)}) collective-permute-start(bf16[64,1,1536]{0,2,1:T(8,128)(2,1)} %collective-permute-done.13), channel_id=1, source_target_pairs={{0,480},{32,0},{64,32},{96,64},{128,96},{160,128},{192,160},{224,1... | collective-permute-start | bytes 589832 | tf_op jit(solution)/shard_map/ppermute | solution.py:83
  118.1 12.6 %collective-permute-start.7 = (bf16[64,1,1536]{0,2,1:T(8,128)(2,1)}, bf16[64,1,1536]{0,2,1:T(8,128)(2,1)}, u32[]{:S(2)}, u32[]{:S(2)}) collective-permute-start(bf16[64,1,1536]{0,2,1:T(8,128)(2,1)} %collective-permute-done.6), channel_id=1, source_target_pairs={{0,32},{32,64},{64,96},{96,128},{128,160},{160,192},{192,224},{224... | collective-permute-start | bytes 589832 | tf_op jit(solution)/shard_map/ppermute | solution.py:81
  147.2 23.5 %all-to-all-start.1 = ((bf16[32,1,16,1024]{3,2,1,0:T(8,128)(2,1)}), bf16[32,1,16,1024]{3,2,1,0:T(8,128)(2,1)S(1)}, u32[]{:S(2)}, u32[]{:S(2)}) async-start(bf16[32,1,16,1024]{3,2,1,0:T(8,128)(2,1)} %bitcast.14), calls=%async_computation.1 | async-start | bytes 2097152 | tf_op jit(solution)/shard_map/all_to_all | solution.py:69
  154.6 102.7 %reduce-scatter.4.cloned.1.call-start = ((), (), s32[]{:S(2)}) async-start(), calls=%async_computation.7 | async-start | bytes 3342336
  189.8 22.0 %all-to-all-start.4 = ((bf16[32,1,16,1024]{3,2,1,0:T(8,128)(2,1)}), bf16[32,1,16,1024]{3,2,1,0:T(8,128)(2,1)}, u32[]{:S(2)}, u32[]{:S(2)}) async-start(bf16[32,1,16,1024]{3,2,1,0:T(8,128)(2,1)} %copy.109), calls=%async_computation.4 | async-start | bytes 2097152 | tf_op jit(solution)/shard_map/all_to_all | solution.py:107
  195.6 203.9 %all-reduce.2.cloned.1.call-start = ((), (), s32[]{:S(2)}) async-start(), calls=%async_computation.6 | async-start | bytes 3145728 | tf_op jit(solution)/shard_map/psum | solution.py:123
  211.8 21.3 %all-to-all-start.3 = ((bf16[32,1,16,1024]{3,2,1,0:T(8,128)(2,1)}), bf16[32,1,16,1024]{3,2,1,0:T(8,128)(2,1)S(1)}, u32[]{:S(2)}, u32[]{:S(2)}) async-start(bf16[32,1,16,1024]{3,2,1,0:T(8,128)(2,1)} %copy.108), calls=%async_computation.3 | async-start | bytes 2097152 | tf_op jit(solution)/shard_map/all_to_all | solution.py:102
  (15 other events, 94.0 us)
Sparse Core Ops, SparseCore 0:
  184.8 72.4 reduce-scatter.3
  260.2 139.3 all-reduce.1
